TPU v7x, 32 devices: a whole 2x2x4 slice. The times are simulated.
32 devices in a mesh: chain: 8 (over z, y), spatial: 2 (over x), dp: 2 (over core).
Axes of the slice: x: 2, y: 2, z: 4, core: 2. Of those that a mesh axis runs over, the one named last changes fastest.
Arguments:
- images: bfloat16 [4, 2, 16, 16, 512], P(None, 'dp', 'spatial'), may hold values from -6 to 6
- cotangent: bfloat16 [4, 2, 16, 16, 512], P(None, 'dp', 'spatial'), may hold values from -0.3125 to 0.3125
- weights: bfloat16 [8, 9, 512, 512], P('chain'), may hold values from -0.046875 to 0.046875
Outputs:
- weight_grads: float32 [8, 9, 512, 512], P('chain', None, ('spatial', 'dp'))
All inputs are finite; a program needn't handle non-finite values.
Results may differ from a plain program's by a relative error of at most 0.015.
Values may be sent and summed in bfloat16 or wider, within the bound.
A program may use at most 64 MiB of HBM per device.

v0:
```python
import jax
import jax.numpy as jnp
from jax import lax
from jax.sharding import PartitionSpec as P


def with_halo(cells, sides, width):
    for axis, dim in sides:
        count = lax.axis_size(axis)
        ends = count - 1
        head = lax.slice_in_dim(cells, 0, width, axis=dim)
        tail = lax.slice_in_dim(cells, cells.shape[dim] - width, cells.shape[dim], axis=dim)
        cells = jnp.concatenate(
            [
                lax.ppermute(tail, axis, [(i, (i + 1) % count) for i in range(ends)]),
                cells,
                lax.ppermute(head, axis, [((i + 1) % count, i) for i in range(ends)]),
            ],
            axis=dim,
        )
    return cells


def passed_along(block, axis, distance):
    devices = range(lax.axis_size(axis))
    route = [(i - distance, i) for i in devices if i - distance in devices]
    return lax.ppermute(block, axis, route)


def patches(padded, rows, cols, reverse):
    offsets = [(a, b) for a in range(3) for b in range(3)]
    if reverse:
        offsets = offsets[::-1]
    parts = [padded[:, a : a + rows, b : b + cols, :] for a, b in offsets]
    return jnp.stack(parts, axis=-2).reshape(-1, 9, padded.shape[-1])


def pad_cols(field):
    return jnp.pad(field, ((0, 0), (0, 0), (1, 1), (0, 0)))


def silu_slope(value):
    sig = jax.nn.sigmoid(value)
    return sig * (1.0 + value * (1.0 - sig))


def shards(images, cotangent, weights):
    micros, imgs, height, width, chans = images.shape
    pixels = imgs * height * width
    sections = lax.axis_size("chain")
    section = lax.axis_index("chain")
    ticks = micros + sections - 1
    kernel = weights[0]
    flat_kernel = kernel.reshape(9 * chans, chans)
    shape_one = (imgs, height, width, chans)

    def forward_tick(tick, carry):
        inbox, saved_x, saved_z = carry
        micro = tick - section
        valid = jnp.logical_and(micro >= 0, micro < micros)
        slot = jnp.clip(micro, 0, micros - 1)
        first = lax.dynamic_index_in_dim(images, slot, 0, keepdims=False)
        source = jnp.where(section == 0, first, inbox)
        rows = with_halo(source, (("spatial", 1),), 1)
        padded = pad_cols(rows)

        def forward_active(operand):
            cols = patches(operand, height, width, False).reshape(-1, 9 * chans)
            state = jnp.dot(cols, flat_kernel, preferred_element_type=jnp.float32)
            output = (source.astype(jnp.float32) + jax.nn.silu(state).reshape(shape_one)).astype(
                jnp.bfloat16
            )
            return (output, state)

        def forward_resting(operand):
            return (jnp.zeros(shape_one, jnp.bfloat16), jnp.zeros((pixels, chans), jnp.float32))

        output, state = lax.cond(valid, forward_active, forward_resting, padded)
        saved_x = jnp.where(
            valid, lax.dynamic_update_index_in_dim(saved_x, padded, slot, 0), saved_x
        )
        saved_z = jnp.where(
            valid, lax.dynamic_update_index_in_dim(saved_z, state, slot, 0), saved_z
        )
        inbox = passed_along(output, "chain", 1)
        return (inbox, saved_x, saved_z)

    start = (
        jnp.zeros(shape_one, jnp.bfloat16),
        jnp.zeros((micros, imgs, height + 2, width + 2, chans), jnp.bfloat16),
        jnp.zeros((micros, pixels, chans), jnp.float32),
    )
    inbox, saved_x, saved_z = lax.fori_loop(0, ticks, forward_tick, start)

    def backward_tick(tick, carry):
        inbox, saved_d = carry
        micro = tick - (sections - 1 - section)
        valid = jnp.logical_and(micro >= 0, micro < micros)
        slot = jnp.clip(micro, 0, micros - 1)
        last = lax.dynamic_index_in_dim(cotangent, slot, 0, keepdims=False)
        upstream = jnp.where(section == sections - 1, last, inbox)
        state = lax.dynamic_index_in_dim(saved_z, slot, 0, keepdims=False)
        delta = (upstream.astype(jnp.float32).reshape(pixels, chans) * silu_slope(state)).astype(
            jnp.bfloat16
        )
        delta = jnp.where(valid, delta, jnp.zeros_like(delta))
        rows = with_halo(delta.reshape(shape_one), (("spatial", 1),), 1)
        padded = pad_cols(rows)

        def backward_active(operand):
            back = patches(operand, height, width, True)
            flow = jnp.einsum("nkc,kdc->nd", back, kernel, preferred_element_type=jnp.float32)
            return (upstream.astype(jnp.float32) + flow.reshape(shape_one)).astype(jnp.bfloat16)

        def backward_resting(operand):
            return jnp.zeros(shape_one, jnp.bfloat16)

        result = lax.cond(valid, backward_active, backward_resting, padded)
        saved_d = jnp.where(
            valid, lax.dynamic_update_index_in_dim(saved_d, delta, slot, 0), saved_d
        )
        inbox = passed_along(result, "chain", -1)
        return (inbox, saved_d)

    begin = (jnp.zeros(shape_one, jnp.bfloat16), jnp.zeros((micros, pixels, chans), jnp.bfloat16))
    inbox, saved_d = lax.fori_loop(0, ticks, backward_tick, begin)
    cols_all = patches(
        saved_x.reshape(micros * imgs, height + 2, width + 2, chans), height, width, False
    )
    cols_all = cols_all.reshape(-1, 9 * chans)
    local_grad = lax.dot_general(
        cols_all,
        saved_d.reshape(-1, chans),
        (((0,), (0,)), ((), ())),
        preferred_element_type=jnp.float32,
    ).reshape(9, chans, chans)
    summed = lax.psum_scatter(
        local_grad.astype(jnp.bfloat16), ("spatial", "dp"), scatter_dimension=1, tiled=True
    ).astype(jnp.float32)
    return summed[None]


def solution(mesh):
    placed = (
        P(None, "dp", "spatial", None, None),
        P(None, "dp", "spatial", None, None),
        P("chain", None, None, None),
    )
    return jax.shard_map(
        shards,
        mesh=mesh,
        in_specs=placed,
        out_specs=P("chain", None, ("spatial", "dp"), None),
        check_vma=False,
    )
```

profile of v0, /device:TPU:1, one launch (start us, length us, event | category | flops | bytes accessed | tf_op | source)
XLA Modules:
  0.0 516.6 jit_solution(7279397532341472872)
XLA Ops:
  6.8 167.2 %while.36 = (s32[]{:T(128)}, bf16[1,8,16,512]{3,2,1,0:T(8,128)(2,1)S(1)}, bf16[4,1,10,18,512]{4,3,2,1,0:T(8,128)(2,1)S(1)}, f32[4,128,512]{2,1,0:T(8,128)S(1)}, ...) while((s32[]{:T(128)}, ...), condition=%wide.region_3.4_spmd, body=%wide.region_0.3_spmd.sunk | while | flops 606873600 | bytes 35803516 | solution.py:93
  77.3 7.3 %collective-permute-start.2 = (bf16[1,8,16,512]{3,2,1,0:T(8,128)(2,1)S(1)}, bf16[1,8,16,512]{3,2,1,0:T(8,128)(2,1)S(1)}, u32[]{:S(2)}, u32[]{:S(2)}) collective-permute-start(bf16[1,8,16,512]{3,2,1,0:T(8,128)(2,1)S(1)} %get-tuple-element.560), channel_id=1, source_target_pairs={{0,4},{4,8},{8,12},{12,16},{16,20},{20,24},{24,28},{1,5},{5,9},{9,... | collective-permute-start | bytes 393224 | tf_op jit(solution)/shard_map/while/body/eval_jaxpr/ppermute | solution.py:27
  93.8 4.6 collective-permute-start.2
  107.6 8.2 %collective-permute-start.2 = (bf16[1,8,16,512]{3,2,1,0:T(8,128)(2,1)S(1)}, bf16[1,8,16,512]{3,2,1,0:T(8,128)(2,1)S(1)}, u32[]{:S(2)}, u32[]{:S(2)}) collective-permute-start(bf16[1,8,16,512]{3,2,1,0:T(8,128)(2,1)S(1)} %get-tuple-element.560), channel_id=1, source_target_pairs={{0,4},{4,8},{8,12},{12,16},{16,20},{20,24},{24,28},{1,5},{5,9},{9,... | collective-permute-start | bytes 393224 | tf_op jit(solution)/shard_map/while/body/eval_jaxpr/ppermute | solution.py:27
  125.0 5.0 collective-permute-start.2
  153.0 5.2 %collective-permute-start.2 = (bf16[1,8,16,512]{3,2,1,0:T(8,128)(2,1)S(1)}, bf16[1,8,16,512]{3,2,1,0:T(8,128)(2,1)S(1)}, u32[]{:S(2)}, u32[]{:S(2)}) collective-permute-start(bf16[1,8,16,512]{3,2,1,0:T(8,128)(2,1)S(1)} %get-tuple-element.560), channel_id=1, source_target_pairs={{0,4},{4,8},{8,12},{12,16},{16,20},{20,24},{24,28},{1,5},{5,9},{9,... | collective-permute-start | bytes 393224 | tf_op jit(solution)/shard_map/while/body/eval_jaxpr/ppermute | solution.py:27
  167.3 4.7 collective-permute-start.2
  182.4 7.3 %copy.6 = bf16[4,8,16,9,512]{4,3,2,1,0:T(8,128)(2,1)S(1)} copy(bf16[4,8,16,9,512]{4,2,1,0,3:T(8,128)(2,1)} %fusion.19) | data formatting | bytes 9437184 | tf_op jit(solution)/shard_map/stack | solution.py:35
  189.7 7.7 %copy.11 = bf16[64,8,9,512]{3,1,2,0:T(8,128)(2,1)} copy(bf16[64,8,9,512]{3,2,1,0:T(8,128)(2,1)S(1)} %bitcast.145) | data formatting | bytes 9437184
  197.4 6.6 %copy.7 = bf16[4608,512]{1,0:T(8,128)(2,1)} copy(bf16[4608,512]{0,1:T(8,128)(2,1)} %bitcast.149) | data formatting | bytes 9437184 | tf_op jit(solution)/shard_map/dot_general | solution.py:131
  204.1 204.9 %while.37 = (s32[]{:T(128)}, bf16[1,8,16,512]{3,2,1,0:T(8,128)(2,1)S(1)}, bf16[4,128,512]{2,1,0:T(8,128)(2,1)S(1)}, s32[]{:T(128)}, pred[]{:T(512)}, /*index=5*/...) while((s32[]{:T(128)}, ...), condition=%wide.region_7.8_spmd, body=%wide.region_4.7_spmd.sunk | while | flops 605913088 | bytes 13271382 | solution.py:126
  212.8 5.7 %collective-permute-done.5 = bf16[1,8,16,512]{3,2,1,0:T(8,128)(2,1)S(1)} collective-permute-done((bf16[1,8,16,512]{3,2,1,0:T(8,128)(2,1)S(1)}, bf16[1,8,16,512]{3,2,1,0:T(8,128)(2,1)S(1)}, u32[]{:S(2)}, u32[]{:S(2)}) %collective-permute-start.5) | collective-permute-done | bytes 131104 | tf_op jit(solution)/shard_map/while/body/eval_jaxpr/ppermute | solution.py:27
  227.2 6.6 %collective-permute-done.5 = bf16[1,8,16,512]{3,2,1,0:T(8,128)(2,1)S(1)} collective-permute-done((bf16[1,8,16,512]{3,2,1,0:T(8,128)(2,1)S(1)}, bf16[1,8,16,512]{3,2,1,0:T(8,128)(2,1)S(1)}, u32[]{:S(2)}, u32[]{:S(2)}) %collective-permute-start.5) | collective-permute-done | bytes 131104 | tf_op jit(solution)/shard_map/while/body/eval_jaxpr/ppermute | solution.py:27
  242.6 5.7 %collective-permute-done.5 = bf16[1,8,16,512]{3,2,1,0:T(8,128)(2,1)S(1)} collective-permute-done((bf16[1,8,16,512]{3,2,1,0:T(8,128)(2,1)S(1)}, bf16[1,8,16,512]{3,2,1,0:T(8,128)(2,1)S(1)}, u32[]{:S(2)}, u32[]{:S(2)}) %collective-permute-start.5) | collective-permute-done | bytes 131104 | tf_op jit(solution)/shard_map/while/body/eval_jaxpr/ppermute | solution.py:27
  257.0 5.7 %collective-permute-done.5 = bf16[1,8,16,512]{3,2,1,0:T(8,128)(2,1)S(1)} collective-permute-done((bf16[1,8,16,512]{3,2,1,0:T(8,128)(2,1)S(1)}, bf16[1,8,16,512]{3,2,1,0:T(8,128)(2,1)S(1)}, u32[]{:S(2)}, u32[]{:S(2)}) %collective-permute-start.5) | collective-permute-done | bytes 131104 | tf_op jit(solution)/shard_map/while/body/eval_jaxpr/ppermute | solution.py:27
  271.4 6.8 %collective-permute-done.5 = bf16[1,8,16,512]{3,2,1,0:T(8,128)(2,1)S(1)} collective-permute-done((bf16[1,8,16,512]{3,2,1,0:T(8,128)(2,1)S(1)}, bf16[1,8,16,512]{3,2,1,0:T(8,128)(2,1)S(1)}, u32[]{:S(2)}, u32[]{:S(2)}) %collective-permute-start.5) | collective-permute-done | bytes 131104 | tf_op jit(solution)/shard_map/while/body/eval_jaxpr/ppermute | solution.py:27
  286.9 6.6 %collective-permute-done.5 = bf16[1,8,16,512]{3,2,1,0:T(8,128)(2,1)S(1)} collective-permute-done((bf16[1,8,16,512]{3,2,1,0:T(8,128)(2,1)S(1)}, bf16[1,8,16,512]{3,2,1,0:T(8,128)(2,1)S(1)}, u32[]{:S(2)}, u32[]{:S(2)}) %collective-permute-start.5) | collective-permute-done | bytes 131104 | tf_op jit(solution)/shard_map/while/body/eval_jaxpr/ppermute | solution.py:27
  302.3 33.2 %collective-permute-done.5 = bf16[1,8,16,512]{3,2,1,0:T(8,128)(2,1)S(1)} collective-permute-done((bf16[1,8,16,512]{3,2,1,0:T(8,128)(2,1)S(1)}, bf16[1,8,16,512]{3,2,1,0:T(8,128)(2,1)S(1)}, u32[]{:S(2)}, u32[]{:S(2)}) %collective-permute-start.5) | collective-permute-done | bytes 131104 | tf_op jit(solution)/shard_map/while/body/eval_jaxpr/ppermute | solution.py:27
  348.5 5.3 %collective-permute-done.5 = bf16[1,8,16,512]{3,2,1,0:T(8,128)(2,1)S(1)} collective-permute-done((bf16[1,8,16,512]{3,2,1,0:T(8,128)(2,1)S(1)}, bf16[1,8,16,512]{3,2,1,0:T(8,128)(2,1)S(1)}, u32[]{:S(2)}, u32[]{:S(2)}) %collective-permute-start.5) | collective-permute-done | bytes 131104 | tf_op jit(solution)/shard_map/while/body/eval_jaxpr/ppermute | solution.py:27
  366.8 6.2 %collective-permute-done.5 = bf16[1,8,16,512]{3,2,1,0:T(8,128)(2,1)S(1)} collective-permute-done((bf16[1,8,16,512]{3,2,1,0:T(8,128)(2,1)S(1)}, bf16[1,8,16,512]{3,2,1,0:T(8,128)(2,1)S(1)}, u32[]{:S(2)}, u32[]{:S(2)}) %collective-permute-start.5) | collective-permute-done | bytes 131104 | tf_op jit(solution)/shard_map/while/body/eval_jaxpr/ppermute | solution.py:27
  386.0 5.6 %collective-permute-done.5 = bf16[1,8,16,512]{3,2,1,0:T(8,128)(2,1)S(1)} collective-permute-done((bf16[1,8,16,512]{3,2,1,0:T(8,128)(2,1)S(1)}, bf16[1,8,16,512]{3,2,1,0:T(8,128)(2,1)S(1)}, u32[]{:S(2)}, u32[]{:S(2)}) %collective-permute-start.5) | collective-permute-done | bytes 131104 | tf_op jit(solution)/shard_map/while/body/eval_jaxpr/ppermute | solution.py:27
  404.6 4.4 collective-permute-done.5
  409.0 6.6 %convolution_convert_fusion = bf16[9,512,512]{2,1,0:T(8,128)(2,1)} fusion(bf16[9,512,512]{2,1,0:T(8,128)(2,1)} %bitcast.159, bf16[512,512,1]{1,0,2:T(8,128)(2,1)S(1)} %bitcast.160), kind=kOutput, calls=%fused_computation.51 | convolution fusion | flops 2418278400 | bytes 9961472 | tf_op jit(solution)/shard_map/dot_general | solution.py:131
  415.6 91.2 %reduce-scatter.2.cloned.1.call-done = bf16[9,128,512]{2,1,0:T(8,128)(2,1)} async-done(((bf16[9,512,512]{2,1,0:T(8,128)(2,1)}), bf16[9,128,512]{2,1,0:T(8,128)(2,1)}) %reduce-scatter.2.cloned.1.call-update) | async-done | bytes 1179664 | tf_op jit(solution)/shard_map/reduce_scatter | solution.py:137
  (389 shorter events, 286.4 us)
Async XLA Ops:
  6.5 500.2 %reduce-scatter.2.cloned.1.call-start = ((), (), s32[]{:S(2)}) async-start(), calls=%async_computation.1 | async-start | bytes 5898240 | tf_op jit(solution)/shard_map/reduce_scatter | solution.py:137
  31.5 5.7 %collective-permute-start.2 = (bf16[1,8,16,512]{3,2,1,0:T(8,128)(2,1)S(1)}, bf16[1,8,16,512]{3,2,1,0:T(8,128)(2,1)S(1)}, u32[]{:S(2)}, u32[]{:S(2)}) collective-permute-start(bf16[1,8,16,512]{3,2,1,0:T(8,128)(2,1)S(1)} %get-tuple-element.560), channel_id=1, source_target_pairs={{0,4},{4,8},{8,12},{12,16},{16,20},{20,24},{24,28},{1,5},{5,9},{9,... | collective-permute-start | bytes 393224 | tf_op jit(solution)/shard_map/while/body/eval_jaxpr/ppermute | solution.py:27
  47.9 5.7 %collective-permute-start.2 = (bf16[1,8,16,512]{3,2,1,0:T(8,128)(2,1)S(1)}, bf16[1,8,16,512]{3,2,1,0:T(8,128)(2,1)S(1)}, u32[]{:S(2)}, u32[]{:S(2)}) collective-permute-start(bf16[1,8,16,512]{3,2,1,0:T(8,128)(2,1)S(1)} %get-tuple-element.560), channel_id=1, source_target_pairs={{0,4},{4,8},{8,12},{12,16},{16,20},{20,24},{24,28},{1,5},{5,9},{9,... | collective-permute-start | bytes 393224 | tf_op jit(solution)/shard_map/while/body/eval_jaxpr/ppermute | solution.py:27
  64.4 5.7 %collective-permute-start.2 = (bf16[1,8,16,512]{3,2,1,0:T(8,128)(2,1)S(1)}, bf16[1,8,16,512]{3,2,1,0:T(8,128)(2,1)S(1)}, u32[]{:S(2)}, u32[]{:S(2)}) collective-permute-start(bf16[1,8,16,512]{3,2,1,0:T(8,128)(2,1)S(1)} %get-tuple-element.560), channel_id=1, source_target_pairs={{0,4},{4,8},{8,12},{12,16},{16,20},{20,24},{24,28},{1,5},{5,9},{9,... | collective-permute-start | bytes 393224 | tf_op jit(solution)/shard_map/while/body/eval_jaxpr/ppermute | solution.py:27
  77.3 9.2 %collective-permute-start.2 = (bf16[1,8,16,512]{3,2,1,0:T(8,128)(2,1)S(1)}, bf16[1,8,16,512]{3,2,1,0:T(8,128)(2,1)S(1)}, u32[]{:S(2)}, u32[]{:S(2)}) collective-permute-start(bf16[1,8,16,512]{3,2,1,0:T(8,128)(2,1)S(1)} %get-tuple-element.560), channel_id=1, source_target_pairs={{0,4},{4,8},{8,12},{12,16},{16,20},{20,24},{24,28},{1,5},{5,9},{9,... | collective-permute-start | bytes 393224 | tf_op jit(solution)/shard_map/while/body/eval_jaxpr/ppermute | solution.py:27
  93.8 6.6 %collective-permute-start.2 = (bf16[1,8,16,512]{3,2,1,0:T(8,128)(2,1)S(1)}, bf16[1,8,16,512]{3,2,1,0:T(8,128)(2,1)S(1)}, u32[]{:S(2)}, u32[]{:S(2)}) collective-permute-start(bf16[1,8,16,512]{3,2,1,0:T(8,128)(2,1)S(1)} %get-tuple-element.560), channel_id=1, source_target_pairs={{0,4},{4,8},{8,12},{12,16},{16,20},{20,24},{24,28},{1,5},{5,9},{9,... | collective-permute-start | bytes 393224 | tf_op jit(solution)/shard_map/while/body/eval_jaxpr/ppermute | solution.py:27
  107.6 10.1 %collective-permute-start.2 = (bf16[1,8,16,512]{3,2,1,0:T(8,128)(2,1)S(1)}, bf16[1,8,16,512]{3,2,1,0:T(8,128)(2,1)S(1)}, u32[]{:S(2)}, u32[]{:S(2)}) collective-permute-start(bf16[1,8,16,512]{3,2,1,0:T(8,128)(2,1)S(1)} %get-tuple-element.560), channel_id=1, source_target_pairs={{0,4},{4,8},{8,12},{12,16},{16,20},{20,24},{24,28},{1,5},{5,9},{9,... | collective-permute-start | bytes 393224 | tf_op jit(solution)/shard_map/while/body/eval_jaxpr/ppermute | solution.py:27
  125.0 7.4 %collective-permute-start.2 = (bf16[1,8,16,512]{3,2,1,0:T(8,128)(2,1)S(1)}, bf16[1,8,16,512]{3,2,1,0:T(8,128)(2,1)S(1)}, u32[]{:S(2)}, u32[]{:S(2)}) collective-permute-start(bf16[1,8,16,512]{3,2,1,0:T(8,128)(2,1)S(1)} %get-tuple-element.560), channel_id=1, source_target_pairs={{0,4},{4,8},{8,12},{12,16},{16,20},{20,24},{24,28},{1,5},{5,9},{9,... | collective-permute-start | bytes 393224 | tf_op jit(solution)/shard_map/while/body/eval_jaxpr/ppermute | solution.py:27
  133.3 5.4 %collective-permute-start = (bf16[1,1,16,512]{3,2,1,0:T(8,128)(2,1)S(1)}, bf16[1,1,16,512]{3,2,1,0:T(8,128)(2,1)S(1)}, u32[]{:S(2)}, u32[]{:S(2)}) collective-permute-start(bf16[1,1,16,512]{3,2,1,0:T(8,128)(2,1)S(1)} %get-tuple-element.558), channel_id=1, source_target_pairs={{2,0},{3,1},{6,4},{7,5},{10,8},{11,9},{14,12},{15,13},{18,16},{19,... | collective-permute-start | bytes 49160 | tf_op jit(solution)/shard_map/while/body/eval_jaxpr/ppermute | solution.py:17
  139.7 6.1 %collective-permute-start.2 = (bf16[1,8,16,512]{3,2,1,0:T(8,128)(2,1)S(1)}, bf16[1,8,16,512]{3,2,1,0:T(8,128)(2,1)S(1)}, u32[]{:S(2)}, u32[]{:S(2)}) collective-permute-start(bf16[1,8,16,512]{3,2,1,0:T(8,128)(2,1)S(1)} %get-tuple-element.560), channel_id=1, source_target_pairs={{0,4},{4,8},{8,12},{12,16},{16,20},{20,24},{24,28},{1,5},{5,9},{9,... | collective-permute-start | bytes 393224 | tf_op jit(solution)/shard_map/while/body/eval_jaxpr/ppermute | solution.py:27
  153.0 7.1 %collective-permute-start.2 = (bf16[1,8,16,512]{3,2,1,0:T(8,128)(2,1)S(1)}, bf16[1,8,16,512]{3,2,1,0:T(8,128)(2,1)S(1)}, u32[]{:S(2)}, u32[]{:S(2)}) collective-permute-start(bf16[1,8,16,512]{3,2,1,0:T(8,128)(2,1)S(1)} %get-tuple-element.560), channel_id=1, source_target_pairs={{0,4},{4,8},{8,12},{12,16},{16,20},{20,24},{24,28},{1,5},{5,9},{9,... | collective-permute-start | bytes 393224 | tf_op jit(solution)/shard_map/while/body/eval_jaxpr/ppermute | solution.py:27
  167.3 6.6 %collective-permute-start.2 = (bf16[1,8,16,512]{3,2,1,0:T(8,128)(2,1)S(1)}, bf16[1,8,16,512]{3,2,1,0:T(8,128)(2,1)S(1)}, u32[]{:S(2)}, u32[]{:S(2)}) collective-permute-start(bf16[1,8,16,512]{3,2,1,0:T(8,128)(2,1)S(1)} %get-tuple-element.560), channel_id=1, source_target_pairs={{0,4},{4,8},{8,12},{12,16},{16,20},{20,24},{24,28},{1,5},{5,9},{9,... | collective-permute-start | bytes 393224 | tf_op jit(solution)/shard_map/while/body/eval_jaxpr/ppermute | solution.py:27
  211.5 7.0 %collective-permute-start.5 = (bf16[1,8,16,512]{3,2,1,0:T(8,128)(2,1)S(1)}, bf16[1,8,16,512]{3,2,1,0:T(8,128)(2,1)S(1)}, u32[]{:S(2)}, u32[]{:S(2)}) collective-permute-start(bf16[1,8,16,512]{3,2,1,0:T(8,128)(2,1)S(1)} %get-tuple-element.651), channel_id=1, source_target_pairs={{4,0},{8,4},{12,8},{16,12},{20,16},{24,20},{28,24},{5,1},{9,5},{13... | collective-permute-start | bytes 393224 | tf_op jit(solution)/shard_map/while/body/eval_jaxpr/ppermute | solution.py:27
  225.9 7.9 %collective-permute-start.5 = (bf16[1,8,16,512]{3,2,1,0:T(8,128)(2,1)S(1)}, bf16[1,8,16,512]{3,2,1,0:T(8,128)(2,1)S(1)}, u32[]{:S(2)}, u32[]{:S(2)}) collective-permute-start(bf16[1,8,16,512]{3,2,1,0:T(8,128)(2,1)S(1)} %get-tuple-element.651), channel_id=1, source_target_pairs={{4,0},{8,4},{12,8},{16,12},{20,16},{24,20},{28,24},{5,1},{9,5},{13... | collective-permute-start | bytes 393224 | tf_op jit(solution)/shard_map/while/body/eval_jaxpr/ppermute | solution.py:27
  241.2 7.0 %collective-permute-start.5 = (bf16[1,8,16,512]{3,2,1,0:T(8,128)(2,1)S(1)}, bf16[1,8,16,512]{3,2,1,0:T(8,128)(2,1)S(1)}, u32[]{:S(2)}, u32[]{:S(2)}) collective-permute-start(bf16[1,8,16,512]{3,2,1,0:T(8,128)(2,1)S(1)} %get-tuple-element.651), channel_id=1, source_target_pairs={{4,0},{8,4},{12,8},{16,12},{20,16},{24,20},{28,24},{5,1},{9,5},{13... | collective-permute-start | bytes 393224 | tf_op jit(solution)/shard_map/while/body/eval_jaxpr/ppermute | solution.py:27
  255.6 7.0 %collective-permute-start.5 = (bf16[1,8,16,512]{3,2,1,0:T(8,128)(2,1)S(1)}, bf16[1,8,16,512]{3,2,1,0:T(8,128)(2,1)S(1)}, u32[]{:S(2)}, u32[]{:S(2)}) collective-permute-start(bf16[1,8,16,512]{3,2,1,0:T(8,128)(2,1)S(1)} %get-tuple-element.651), channel_id=1, source_target_pairs={{4,0},{8,4},{12,8},{16,12},{20,16},{24,20},{28,24},{5,1},{9,5},{13... | collective-permute-start | bytes 393224 | tf_op jit(solution)/shard_map/while/body/eval_jaxpr/ppermute | solution.py:27
  270.1 8.2 %collective-permute-start.5 = (bf16[1,8,16,512]{3,2,1,0:T(8,128)(2,1)S(1)}, bf16[1,8,16,512]{3,2,1,0:T(8,128)(2,1)S(1)}, u32[]{:S(2)}, u32[]{:S(2)}) collective-permute-start(bf16[1,8,16,512]{3,2,1,0:T(8,128)(2,1)S(1)} %get-tuple-element.651), channel_id=1, source_target_pairs={{4,0},{8,4},{12,8},{16,12},{20,16},{24,20},{28,24},{5,1},{9,5},{13... | collective-permute-start | bytes 393224 | tf_op jit(solution)/shard_map/while/body/eval_jaxpr/ppermute | solution.py:27
  285.6 8.0 %collective-permute-start.5 = (bf16[1,8,16,512]{3,2,1,0:T(8,128)(2,1)S(1)}, bf16[1,8,16,512]{3,2,1,0:T(8,128)(2,1)S(1)}, u32[]{:S(2)}, u32[]{:S(2)}) collective-permute-start(bf16[1,8,16,512]{3,2,1,0:T(8,128)(2,1)S(1)} %get-tuple-element.651), channel_id=1, source_target_pairs={{4,0},{8,4},{12,8},{16,12},{20,16},{24,20},{28,24},{5,1},{9,5},{13... | collective-permute-start | bytes 393224 | tf_op jit(solution)/shard_map/while/body/eval_jaxpr/ppermute | solution.py:27
  301.0 34.6 %collective-permute-start.5 = (bf16[1,8,16,512]{3,2,1,0:T(8,128)(2,1)S(1)}, bf16[1,8,16,512]{3,2,1,0:T(8,128)(2,1)S(1)}, u32[]{:S(2)}, u32[]{:S(2)}) collective-permute-start(bf16[1,8,16,512]{3,2,1,0:T(8,128)(2,1)S(1)} %get-tuple-element.651), channel_id=1, source_target_pairs={{4,0},{8,4},{12,8},{16,12},{20,16},{24,20},{28,24},{5,1},{9,5},{13... | collective-permute-start | bytes 393224 | tf_op jit(solution)/shard_map/while/body/eval_jaxpr/ppermute | solution.py:27
  347.2 6.6 %collective-permute-start.5 = (bf16[1,8,16,512]{3,2,1,0:T(8,128)(2,1)S(1)}, bf16[1,8,16,512]{3,2,1,0:T(8,128)(2,1)S(1)}, u32[]{:S(2)}, u32[]{:S(2)}) collective-permute-start(bf16[1,8,16,512]{3,2,1,0:T(8,128)(2,1)S(1)} %get-tuple-element.651), channel_id=1, source_target_pairs={{4,0},{8,4},{12,8},{16,12},{20,16},{24,20},{28,24},{5,1},{9,5},{13... | collective-permute-start | bytes 393224 | tf_op jit(solution)/shard_map/while/body/eval_jaxpr/ppermute | solution.py:27
  365.5 7.5 %collective-permute-start.5 = (bf16[1,8,16,512]{3,2,1,0:T(8,128)(2,1)S(1)}, bf16[1,8,16,512]{3,2,1,0:T(8,128)(2,1)S(1)}, u32[]{:S(2)}, u32[]{:S(2)}) collective-permute-start(bf16[1,8,16,512]{3,2,1,0:T(8,128)(2,1)S(1)} %get-tuple-element.651), channel_id=1, source_target_pairs={{4,0},{8,4},{12,8},{16,12},{20,16},{24,20},{28,24},{5,1},{9,5},{13... | collective-permute-start | bytes 393224 | tf_op jit(solution)/shard_map/while/body/eval_jaxpr/ppermute | solution.py:27
  374.2 5.3 %collective-permute-start.3 = (bf16[1,1,16,512]{3,2,1,0:T(8,128)(2,1)S(1)}, bf16[1,1,16,512]{3,2,1,0:T(8,128)(2,1)S(1)}, u32[]{:S(2)}, u32[]{:S(2)}) collective-permute-start(bf16[1,1,16,512]{3,2,1,0:T(8,128)(2,1)S(1)} %get-tuple-element.572), channel_id=1, source_target_pairs={{2,0},{3,1},{6,4},{7,5},{10,8},{11,9},{14,12},{15,13},{18,16},{19,... | collective-permute-start | bytes 49160 | tf_op jit(solution)/shard_map/while/body/eval_jaxpr/ppermute | solution.py:17
  384.7 7.0 %collective-permute-start.5 = (bf16[1,8,16,512]{3,2,1,0:T(8,128)(2,1)S(1)}, bf16[1,8,16,512]{3,2,1,0:T(8,128)(2,1)S(1)}, u32[]{:S(2)}, u32[]{:S(2)}) collective-permute-start(bf16[1,8,16,512]{3,2,1,0:T(8,128)(2,1)S(1)} %get-tuple-element.651), channel_id=1, source_target_pairs={{4,0},{8,4},{12,8},{16,12},{20,16},{24,20},{28,24},{5,1},{9,5},{13... | collective-permute-start | bytes 393224 | tf_op jit(solution)/shard_map/while/body/eval_jaxpr/ppermute | solution.py:27
  403.3 5.7 %collective-permute-start.5 = (bf16[1,8,16,512]{3,2,1,0:T(8,128)(2,1)S(1)}, bf16[1,8,16,512]{3,2,1,0:T(8,128)(2,1)S(1)}, u32[]{:S(2)}, u32[]{:S(2)}) collective-permute-start(bf16[1,8,16,512]{3,2,1,0:T(8,128)(2,1)S(1)} %get-tuple-element.651), channel_id=1, source_target_pairs={{4,0},{8,4},{12,8},{16,12},{20,16},{24,20},{28,24},{5,1},{9,5},{13... | collective-permute-start | bytes 393224 | tf_op jit(solution)/shard_map/while/body/eval_jaxpr/ppermute | solution.py:27
  (47 other events, 225.2 us)
Sparse Core Ops, SparseCore 0:
  415.7 90.9 reduce-scatter.1
where the time goes:
time: 520 us; the launch traced here: 517 us
  waiting for transfers between devices  221 us (42%)
  starting transfers between devices  182 us (35%)
  local copies, waits for them, and re-layouts  42 us (8%)
  other arithmetic  29.8 us (6%)
  matrix products  25.7 us (5%)
  between operations  13.4 us (3%)
    ppermute x22, waiting for transfers between devices, passed_along(): return lax.ppermute(block, axis, route)  111 us
    reduce_scatter x1, waiting for transfers between devices, shards(): lax.psum_scatter(local_grad.astype(jnp.bfloat16), ('spatial', 'dp'), scat...  91.2 us
    ppermute x22, starting transfers between devices, with_halo(): lax.ppermute(tail, axis, [(i, (i + 1) % count) for i in range(ends)])  87.7 us
    ppermute x22, starting transfers between devices, passed_along(): return lax.ppermute(block, axis, route)  65.9 us
    ppermute x22, starting transfers between devices, with_halo(): lax.ppermute(head, axis, [((i + 1) % count, i) for i in range(ends)])  28.4 us
    ppermute x22, waiting for transfers between devices, with_halo(): lax.ppermute(tail, axis, [(i, (i + 1) % count) for i in range(ends)])  18.4 us
    dot_general x4, matrix products, backward_active(): jnp.einsum('nkc,kdc->nd', back, kernel, preferred_element_type=jnp.float32)  15.8 us
    unnamed x9, local copies, waits for them, and re-layouts  15.2 us
  transfers between devices with their start and end apart: 67, of which 45 were waited for; matrix products, arithmetic and copies ran while one was open for 1% of the time, Pallas kernels for 0%

commit v1 on v0

--- a/solution.py
+++ b/solution.py
@@ -1,6 +1,8 @@
 import jax
 import jax.numpy as jnp
 from jax import lax
+from jax.experimental import pallas as pl
+from jax.experimental.pallas import tpu as pltpu
 from jax.sharding import PartitionSpec as P
 
 
@@ -139,6 +141,400 @@
     ).astype(jnp.float32)
     return summed[None]
 
+LANES = 128
+MESH = pl.DeviceIdType.MESH
+
+
+def pipeline_kernel(
+    images, cotangent, weights, out,
+    w, wt, xin, xout, gin, gout, slope, dall, xs, xt, acc, cat, grad,
+    w_sem, loc_sem, out_sem,
+    f_send, x_send, x_recv, xh_send, xh_recv,
+    g_send, g_recv, gh_send, gh_recv,
+    s_send, s_recv, xs_send, xs_recv, d_send, d_recv,
+):
+    micros, quarters, padded_rows, cols, _ = xin.shape
+    rows = padded_rows - 2
+    pixels = rows * cols
+    chans = quarters * LANES
+    half = chans // 2
+    hq = quarters // 2
+    stage = lax.axis_index("chain")
+    last = lax.axis_size("chain") - 1
+    sp = lax.axis_index("spatial")
+    dp = lax.axis_index("dp")
+    osp, odp = 1 - sp, 1 - dp
+    me = sp * 2 + dp
+    mates = ((sp, odp), (osp, dp), (osp, odp))
+    edge_src = (rows - 1) * osp
+    edge_dst = (rows + 1) * sp
+
+    def remote(src, dst, send, recv, chain, spatial, core):
+        return pltpu.make_async_remote_copy(
+            src_ref=src, dst_ref=dst, send_sem=send, recv_sem=recv,
+            device_id=(chain, spatial, core), device_id_type=MESH,
+        )
+
+    def x_main(m, c):
+        return remote(
+            xout.at[m, pl.ds(c * hq, hq)], xin.at[m, pl.ds(c * hq, hq), pl.ds(1, rows)],
+            x_send.at[m, c], x_recv.at[m, c], stage + 1, sp, dp)
+
+    def x_edge(m, c):
+        return remote(
+            xout.at[m, pl.ds(c * hq, hq), pl.ds(edge_src, 1)],
+            xin.at[m, pl.ds(c * hq, hq), pl.ds(edge_dst, 1)],
+            xh_send.at[m, c], xh_recv.at[m, c], stage + 1, osp, dp)
+
+    def x_first(m, c):
+        return remote(
+            xin.at[m, pl.ds(c * hq, hq), pl.ds(1 + edge_src, 1)],
+            xin.at[m, pl.ds(c * hq, hq), pl.ds(edge_dst, 1)],
+            f_send.at[m, c], xh_recv.at[m, c], stage, osp, dp)
+
+    def g_main(m, c):
+        return remote(
+            gout.at[m, pl.ds(c * hq, hq)], gin.at[m, pl.ds(c * hq, hq), pl.ds(1, rows)],
+            g_send.at[m, c], g_recv.at[m, c], stage - 1, sp, dp)
+
+    def g_edge(m, c):
+        return remote(
+            gout.at[m, pl.ds(c * hq, hq), pl.ds(edge_src, 1)],
+            gin.at[m, pl.ds(c * hq, hq), pl.ds(edge_dst, 1)],
+            gh_send.at[m, c], gh_recv.at[m, c], stage - 1, osp, dp)
+
+    def g_first(m, c):
+        return remote(
+            gin.at[m, pl.ds(c * hq, hq), pl.ds(1 + edge_src, 1)],
+            gin.at[m, pl.ds(c * hq, hq), pl.ds(edge_dst, 1)],
+            f_send.at[m, c], gh_recv.at[m, c], stage, osp, dp)
+
+    def slope_edge(m):
+        return remote(
+            slope.at[m, :, pl.ds(1 + edge_src, 1)], slope.at[m, :, pl.ds(edge_dst, 1)],
+            s_send.at[m], s_recv.at[m], stage, osp, dp)
+
+    def x_slice(m, j):
+        a, b = mates[j]
+        return remote(
+            xin.at[m, a * 2 + b, pl.ds(1, rows)], xs.at[m, me],
+            xs_send.at[m, j], xs_recv.at[m, j], stage, a, b)
+
+    def d_block(m, c, j):
+        a, b = ((sp, odp), (osp, dp), (sp, odp))[j]
+        owner = me if j < 2 else osp * 2 + dp
+        block = dall.at[m, owner, pl.ds(c * hq, hq)]
+        return remote(block, block, d_send.at[m, j, c], d_recv.at[m, j, c], stage, a, b)
+
+    def local_in(array, buffer, m, q):
+        return pltpu.make_async_copy(
+            array.at[m, :, :, pl.ds(q * LANES, LANES)], buffer.at[m, q, pl.ds(1, rows)],
+            loc_sem.at[m, q])
+
+    w_copy = pltpu.make_async_copy(weights, w, w_sem)
+    w_copy.start()
+
+    @pl.when(stage == 0)
+    def _():
+        for m in range(micros):
+            for q in range(quarters):
+                local_in(images, xin, m, q).start()
+
+    @pl.when(stage == last)
+    def _():
+        for m in range(micros):
+            for q in range(quarters):
+                local_in(cotangent, gin, m, q).start()
+
+    barrier = pltpu.get_barrier_semaphore()
+
+    def greet(chain, spatial, core):
+        pl.semaphore_signal(barrier, inc=1, device_id=(chain, spatial, core), device_id_type=MESH)
+
+    for a, b in mates:
+        greet(stage, a, b)
+
+    @pl.when(stage > 0)
+    def _():
+        greet(stage - 1, sp, dp)
+        greet(stage - 1, osp, dp)
+
+    @pl.when(stage < last)
+    def _():
+        greet(stage + 1, sp, dp)
+        greet(stage + 1, osp, dp)
+
+    zero_row = (rows + 1) * sp
+    blank = jnp.zeros((micros, quarters, 1, cols, LANES), jnp.float32)
+    xin[:, :, pl.ds(zero_row, 1)] = blank.astype(xin.dtype)
+    gin[:, :, pl.ds(zero_row, 1)] = blank.astype(gin.dtype)
+    slope[:, :, pl.ds(zero_row, 1)] = blank
+    grad[...] = jnp.zeros_like(grad)
+
+    around = jnp.where(stage > 0, 2, 0) + jnp.where(stage < last, 2, 0)
+    pl.semaphore_wait(barrier, 3 + around)
+
+    @pl.when(stage == 0)
+    def _():
+        for m in range(micros):
+            for q in range(quarters):
+                local_in(images, xin, m, q).wait()
+            for c in range(2):
+                x_first(m, c).start()
+
+    @pl.when(stage == last)
+    def _():
+        for m in range(micros):
+            for q in range(quarters):
+                local_in(cotangent, gin, m, q).wait()
+            for c in range(2):
+                g_first(m, c).start()
+
+    w_copy.wait()
+
+    @pl.when(stage > 0)
+    def _():
+        @pl.loop(0, 9)
+        def _(k):
+            wt[k] = w[8 - k].T
+
+    def column_shifts(value):
+        n = value.shape[0]
+        col = lax.broadcasted_iota(jnp.int32, value.shape, 0) % cols
+        before = jnp.where(col == 0, 0.0, pltpu.roll(value, 1, 0))
+        after = jnp.where(col == cols - 1, 0.0, pltpu.roll(value, n - 1, 0))
+        return before, value, after
+
+    def load_half(ref, m, c):
+        parts = [ref[m, c * hq + i].astype(jnp.float32) for i in range(hq)]
+        return jnp.concatenate(parts, axis=-1)
+
+    def spread(value, c):
+        shifted = column_shifts(value.reshape(padded_rows * cols, half))
+        joined = jnp.concatenate([v.astype(cat.dtype) for v in shifted], axis=-1)
+        cat[c] = joined.reshape(padded_rows, cols, 3 * half)
+
+    def product(kernel, c, lo, width):
+        lhs = jnp.concatenate(
+            [cat[c, pl.ds(a, rows)].reshape(pixels, 3 * half) for a in range(3)], axis=-1)
+        rhs = kernel[:, pl.ds(c * half, half), pl.ds(lo, width)].reshape(9 * half, width)
+        return jnp.dot(lhs, rhs, preferred_element_type=jnp.float32)
+
+    def store_half(ref, m, n, first, value):
+        for i in range(hq):
+            part = value[:, i * LANES:(i + 1) * LANES].reshape(rows, cols, LANES)
+            ref[m, n * hq + i, pl.ds(first, rows)] = part.astype(ref.dtype)
+
+    def forward(m):
+        for c in range(2):
+            @pl.when(stage > 0)
+            def _():
+                x_main(m, c).wait_recv()
+
+            x_edge(m, c).wait_recv()
+            spread(load_half(xin, m, c), c)
+            if c == 0:
+                acc[...] = product(w, 0, 0, chans)
+        for n in range(2):
+            z = acc[:, pl.ds(n * half, half)] + product(w, 1, n * half, half)
+            sig = jax.nn.sigmoid(z)
+            own = load_half(xin, m, n)[1:rows + 1].reshape(pixels, half)
+            store_half(xout, m, n, 0, own + z * sig)
+
+            @pl.when(stage < last)
+            def _():
+                x_main(m, n).start()
+                x_edge(m, n).start()
+
+            store_half(slope, m, n, 1, sig * (1.0 + z * (1.0 - sig)))
+        slope_edge(m).start()
+        for j in range(3):
+            x_slice(m, j).start()
+        xs[m, me] = xin[m, me, pl.ds(1, rows)]
+
+    def backward(m):
+        slope_edge(m).wait_recv()
+        for c in range(2):
+            @pl.when(stage < last)
+            def _():
+                g_main(m, c).wait_recv()
+
+            g_edge(m, c).wait_recv()
+
+            d = (load_half(gin, m, c) * load_half(slope, m, c)).astype(dall.dtype)
+            for i in range(hq):
+                dall[m, me, c * hq + i] = d[1:rows + 1, :, i * LANES:(i + 1) * LANES].reshape(
+                    pixels, LANES)
+            @pl.when(stage > 0)
+            def _():
+                spread(d.astype(jnp.float32), c)
+                if c == 0:
+                    acc[...] = product(wt, 0, 0, chans)
+
+            d_block(m, c, 1).start()
+            d_block(m, c, 0).start()
+
+        @pl.when(stage > 0)
+        def _():
+            for n in range(2):
+                own = load_half(gin, m, n)[1:rows + 1].reshape(pixels, half)
+                flow = acc[:, pl.ds(n * half, half)] + product(wt, 1, n * half, half)
+                store_half(gout, m, n, 0, own + flow)
+                g_main(m, n).start()
+                g_edge(m, n).start()
+
+    def prepare(m):
+        for j in range(3):
+            x_slice(m, j).wait_recv()
+        for image in range(2):
+            tall = jnp.concatenate([xs[m, image], xs[m, 2 + image]], axis=0).astype(jnp.float32)
+            blank_row = jnp.zeros((1, cols, LANES), jnp.float32)
+            shifted = column_shifts(tall.reshape(2 * pixels, LANES))
+            for b in range(3):
+                field = jnp.concatenate(
+                    [blank_row, shifted[b].reshape(2 * rows, cols, LANES), blank_row], axis=0)
+                for part in range(2):
+                    for a in range(3):
+                        lo = part * rows + a
+                        block = field[lo:lo + rows].reshape(pixels, LANES)
+                        xt[m, part, 3 * a + b, :, pl.ds(image * LANES, LANES)] = block.T.astype(
+                            xt.dtype)
+
+    def add_grad(m, part):
+        blocks = []
+        for image in range(2):
+            blocks.append(jnp.concatenate(
+                [dall[m, part * 2 + image, q] for q in range(quarters)], axis=-1))
+        rhs = jnp.concatenate(blocks, axis=0)
+        for a in range(3):
+            lhs = xt[m, part, pl.ds(3 * a, 3)].reshape(3 * LANES, 2 * pixels)
+            total = jnp.dot(lhs, rhs, preferred_element_type=jnp.float32)
+            grad[pl.ds(3 * a, 3)] += total.reshape(3, LANES, chans)
+
+    def accumulate(m):
+        for c in range(2):
+            d_block(m, c, 0).wait_recv()
+        add_grad(m, sp)
+        for c in range(2):
+            d_block(m, c, 1).wait_recv()
+            d_block(m, c, 2).start()
+        for c in range(2):
+            d_block(m, c, 2).wait_recv()
+        add_grad(m, osp)
+
+    F, B, Q, W = ([k * micros + i for i in range(micros)] for k in range(4))
+    early = F + Q + [B[0]]
+    for i in range(1, micros):
+        early += [B[i], W[i - 1]]
+    early += [W[-1]]
+    late = F + B + Q + W
+    final = [v for pair in zip(F, B) for v in pair] + Q + W
+
+    @pl.loop(0, 4 * micros)
+    def _(step):
+        code = jnp.int32(0)
+        for i in range(4 * micros):
+            choice = jnp.where(
+                stage == last, final[i], jnp.where(stage * 2 < last + 1, early[i], late[i]))
+            code = jnp.where(step == i, choice, code)
+        kind = code // micros
+        m = code % micros
+
+        @pl.when(kind == 0)
+        def _():
+            forward(m)
+
+        @pl.when(kind == 1)
+        def _():
+            backward(m)
+
+        @pl.when(kind == 2)
+        def _():
+            prepare(m)
+
+        @pl.when(kind == 3)
+        def _():
+            accumulate(m)
+
+    result = pltpu.make_async_copy(grad, out, out_sem)
+    result.start()
+
+    @pl.loop(0, micros)
+    def _(m):
+        slope_edge(m).wait_send()
+        for j in range(3):
+            x_slice(m, j).wait_send()
+        for c in range(2):
+            for j in range(3):
+                d_block(m, c, j).wait_send()
+
+            @pl.when(stage < last)
+            def _():
+                x_main(m, c).wait_send()
+                x_edge(m, c).wait_send()
+
+            @pl.when(stage == 0)
+            def _():
+                x_first(m, c).wait_send()
+
+            @pl.when(stage > 0)
+            def _():
+                g_main(m, c).wait_send()
+                g_edge(m, c).wait_send()
+
+            @pl.when(stage == last)
+            def _():
+                g_first(m, c).wait_send()
+
+    result.wait()
+
+
+def kernel_shards(images, cotangent, weights):
+    micros, imgs, rows, cols, chans = images.shape
+    quarters = chans // LANES
+    pixels = rows * cols
+    bf16, f32 = jnp.bfloat16, jnp.float32
+    dma = pltpu.SemaphoreType.DMA
+    padded = (micros, quarters, rows + 2, cols, LANES)
+    plain = (micros, quarters, rows, cols, LANES)
+    flops = 2 * 3 * micros * pixels * 9 * chans * chans
+    grads = pl.pallas_call(
+        pipeline_kernel,
+        out_shape=jax.ShapeDtypeStruct((9, LANES, chans), f32),
+        in_specs=[pl.BlockSpec(memory_space=pl.ANY)] * 3,
+        out_specs=pl.BlockSpec(memory_space=pl.ANY),
+        scratch_shapes=[
+            pltpu.VMEM((9, chans, chans), bf16),
+            pltpu.VMEM((9, chans, chans), bf16),
+            pltpu.VMEM(padded, bf16),
+            pltpu.VMEM(plain, bf16),
+            pltpu.VMEM(padded, bf16),
+            pltpu.VMEM(plain, bf16),
+            pltpu.VMEM(padded, f32),
+            pltpu.VMEM((micros, 4, quarters, pixels, LANES), bf16),
+            pltpu.VMEM((micros, 4, rows, cols, LANES), bf16),
+            pltpu.VMEM((micros, 2, 9, LANES, 2 * pixels), bf16),
+            pltpu.VMEM((pixels, chans), f32),
+            pltpu.VMEM((2, rows + 2, cols, 3 * chans // 2), bf16),
+            pltpu.VMEM((9, LANES, chans), f32),
+            dma, dma((micros, quarters)), dma,
+            dma((micros, 2)),
+            dma((micros, 2)), dma((micros, 2)), dma((micros, 2)), dma((micros, 2)),
+            dma((micros, 2)), dma((micros, 2)), dma((micros, 2)), dma((micros, 2)),
+            dma((micros,)), dma((micros,)), dma((micros, 3)), dma((micros, 3)),
+            dma((micros, 3, 2)), dma((micros, 3, 2)),
+        ],
+        compiler_params=pltpu.CompilerParams(
+            collective_id=0, has_side_effects=True, vmem_limit_bytes=48 * 2**20),
+        cost_estimate=pl.CostEstimate(
+            flops=flops, bytes_accessed=2 * 9 * chans * chans * 2, transcendentals=0),
+    )(
+        images.reshape(micros, rows, cols, chans),
+        cotangent.reshape(micros, rows, cols, chans),
+        weights.reshape(9, chans, chans),
+    )
+    return grads[None]
+
 
 def solution(mesh):
     placed = (
@@ -146,10 +542,22 @@
         P(None, "dp", "spatial", None, None),
         P("chain", None, None, None),
     )
-    return jax.shard_map(
-        shards,
-        mesh=mesh,
-        in_specs=placed,
-        out_specs=P("chain", None, ("spatial", "dp"), None),
-        check_vma=False,
-    )
+
+    def program(images, cotangent, weights):
+        group = mesh.shape["spatial"] * mesh.shape["dp"]
+        fits = (
+            mesh.shape["spatial"] == 2
+            and mesh.shape["dp"] == 2
+            and images.shape[1] == 2
+            and weights.shape[2] == group * LANES
+            and images.shape[2] * images.shape[3] == 2 * LANES
+        )
+        return jax.shard_map(
+            kernel_shards if fits else shards,
+            mesh=mesh,
+            in_specs=placed,
+            out_specs=P("chain", None, ("spatial", "dp"), None),
+            check_vma=False,
+        )(images, cotangent, weights)
+
+    return program

time: 520 us -> 118 us (0.23)
  waiting for transfers between devices: 221 us -> 0 us
  starting transfers between devices: 182 us -> 0 us
  Pallas kernels: 0 us -> 114 us
  local copies, waits for them, and re-layouts: 42 us -> 3.49 us
  other arithmetic: 29.8 us -> 0 us
  matrix products: 25.7 us -> 0 us
  between operations: 13.4 us -> 0.01 us
    ppermute x66 -> x0, starting transfers between devices: 182 us -> none  [the longest x22 87.7 us: with_halo(): lax.ppermute(tail, axis, [(i, (i + 1) % count) for i in range(ends)])]
    ppermute x66 -> x0, waiting for transfers between devices: 130 us -> none  [the longest x22 111 us: passed_along(): return lax.ppermute(block, axis, route)]
    pallas_call x0 -> x1, Pallas kernels: none -> 114 us  [kernel_shards(): pl.pallas_call(pipeline_kernel, out_shape=jax.ShapeDtypeStruct((9, LANES,...]
    reduce_scatter x1 -> x0, waiting for transfers between devices: 91.2 us -> none  [shards(): lax.psum_scatter(local_grad.astype(jnp.bfloat16), ('spatial', 'dp'), scat...]
    dot_general x9 -> x0, matrix products: 25.7 us -> none  [the longest x4 15.8 us: backward_active(): jnp.einsum('nkc,kdc->nd', back, kernel, preferred_element_type=jnp.float32)]
    select_n x55 -> x0, other arithmetic: 14 us -> none  [the longest x11 10.1 us: forward_tick(): source = jnp.where(section == 0, first, inbox)]
    another operation x30 -> x0, local copies, waits for them, and re-layouts: 12 us -> none  [the longest x14 11.8 us: patches(): return jnp.stack(parts, axis=-2).reshape(-1, 9, padded.shape[-1])]
    unnamed x9 -> x5, local copies, waits for them, and re-layouts: 15.2 us -> 3.49 us
  transfers between devices with their start and end apart: 67 -> 0, of which waited for: 45 -> 0; matrix products, arithmetic and copies ran while one was open for 1% -> 0% of each run, Pallas kernels for 0% -> 0%
where the time goes in v1:
time: 118 us; the launch traced here: 117 us
  Pallas kernels  114 us (97%)
  local copies, waits for them, and re-layouts  3.49 us (3%)
    pallas_call x1, Pallas kernels, kernel_shards(): pl.pallas_call(pipeline_kernel, out_shape=jax.ShapeDtypeStruct((9, LANES,...  114 us
    unnamed x5, local copies, waits for them, and re-layouts  3.49 us

profile of v1, /device:TPU:1, one launch (start us, length us, event | category | flops | bytes accessed | tf_op | source)
XLA Modules:
  0.0 117.4 jit_solution(15594703233645620495)
XLA Ops:
  0.0 0.0 copy-start
  0.0 1.0 copy-done
  1.0 0.0 copy-start.1
  1.0 1.0 copy-done.1
  2.1 113.9 %shard_map.37 = f32[9,128,512]{2,1,0:T(8,128)S(1)} custom-call(bf16[4,8,16,512]{3,2,1,0:T(8,128)(2,1)S(1)} %bitcast.5, bf16[4,8,16,512]{3,2,1,0:T(8,128)(2,1)S(1)} %bitcast.6, bf16[9,512,512]{2,1,0:T(8,128)(2,1)} %bitcast.7), custom_call_target="tpu_custom_call" | custom-call | flops 7247757312 | bytes 9437184 | tf_op jit(solution)/shard_map/pallas_call | solution.py:501
  116.0 1.4 %copy.5 = f32[1,9,128,512]{3,2,1,0:T(8,128)} copy(f32[1,9,128,512]{3,2,1,0:T(8,128)S(1)} %bitcast.4) | data formatting | bytes 4718592
Async XLA Ops:
  0.0 1.0 copy-start
  1.0 1.0 copy-start.1

commit v2 on v1

--- a/solution.py
+++ b/solution.py
@@ -147,9 +147,9 @@
 
 def pipeline_kernel(
     images, cotangent, weights, out,
-    w, wt, xin, xout, gin, gout, slope, dall, xs, xt, acc, cat, grad,
+    w, wt, first, xin, xout, gin, gout, slope, dall, xs, xt, acc, cat, grad,
     w_sem, loc_sem, out_sem,
-    f_send, x_send, x_recv, xh_send, xh_recv,
+    f_send, fm_send, x_send, x_recv, xh_send, xh_recv,
     g_send, g_recv, gh_send, gh_recv,
     s_send, s_recv, xs_send, xs_recv, d_send, d_recv,
 ):
@@ -166,8 +166,9 @@
     osp, odp = 1 - sp, 1 - dp
     me = sp * 2 + dp
     mates = ((sp, odp), (osp, dp), (osp, odp))
-    edge_src = (rows - 1) * osp
-    edge_dst = (rows + 1) * sp
+    edge_src = (rows - 1) * odp
+    edge_dst = (rows + 1) * dp
+    moved = sp != dp
 
     def remote(src, dst, send, recv, chain, spatial, core):
         return pltpu.make_async_remote_copy(
@@ -184,13 +185,18 @@
         return remote(
             xout.at[m, pl.ds(c * hq, hq), pl.ds(edge_src, 1)],
             xin.at[m, pl.ds(c * hq, hq), pl.ds(edge_dst, 1)],
-            xh_send.at[m, c], xh_recv.at[m, c], stage + 1, osp, dp)
-
-    def x_first(m, c):
-        return remote(
-            xin.at[m, pl.ds(c * hq, hq), pl.ds(1 + edge_src, 1)],
-            xin.at[m, pl.ds(c * hq, hq), pl.ds(edge_dst, 1)],
-            f_send.at[m, c], xh_recv.at[m, c], stage, osp, dp)
+            xh_send.at[m, c], xh_recv.at[m, c], stage + 1, sp, odp)
+
+    def first_main(buffer, recv, m, c):
+        return remote(
+            first.at[m, pl.ds(c * hq, hq)], buffer.at[m, pl.ds(c * hq, hq), pl.ds(1, rows)],
+            fm_send.at[m, c], recv.at[m, c], stage, dp, sp)
+
+    def first_edge(buffer, recv, m, c):
+        return remote(
+            first.at[m, pl.ds(c * hq, hq), pl.ds((rows - 1) * osp, 1)],
+            buffer.at[m, pl.ds(c * hq, hq), pl.ds((rows + 1) * sp, 1)],
+            f_send.at[m, c], recv.at[m, c], stage, dp, osp)
 
     def g_main(m, c):
         return remote(
@@ -201,18 +207,12 @@
         return remote(
             gout.at[m, pl.ds(c * hq, hq), pl.ds(edge_src, 1)],
             gin.at[m, pl.ds(c * hq, hq), pl.ds(edge_dst, 1)],
-            gh_send.at[m, c], gh_recv.at[m, c], stage - 1, osp, dp)
-
-    def g_first(m, c):
-        return remote(
-            gin.at[m, pl.ds(c * hq, hq), pl.ds(1 + edge_src, 1)],
-            gin.at[m, pl.ds(c * hq, hq), pl.ds(edge_dst, 1)],
-            f_send.at[m, c], gh_recv.at[m, c], stage, osp, dp)
+            gh_send.at[m, c], gh_recv.at[m, c], stage - 1, sp, odp)
 
     def slope_edge(m):
         return remote(
             slope.at[m, :, pl.ds(1 + edge_src, 1)], slope.at[m, :, pl.ds(edge_dst, 1)],
-            s_send.at[m], s_recv.at[m], stage, osp, dp)
+            s_send.at[m], s_recv.at[m], stage, sp, odp)
 
     def x_slice(m, j):
         a, b = mates[j]
@@ -226,10 +226,26 @@
         block = dall.at[m, owner, pl.ds(c * hq, hq)]
         return remote(block, block, d_send.at[m, j, c], d_recv.at[m, j, c], stage, a, b)
 
-    def local_in(array, buffer, m, q):
+    def local_in(array, m, q):
         return pltpu.make_async_copy(
-            array.at[m, :, :, pl.ds(q * LANES, LANES)], buffer.at[m, q, pl.ds(1, rows)],
-            loc_sem.at[m, q])
+            array.at[m, :, :, pl.ds(q * LANES, LANES)], first.at[m, q], loc_sem.at[m, q])
+
+    def hand_out(array, buffer, recv, edge_recv):
+        for m in range(micros):
+            for q in range(quarters):
+                local_in(array, m, q).wait()
+
+            @pl.when(moved)
+            def _():
+                for c in range(2):
+                    first_main(buffer, recv, m, c).start()
+
+            for c in range(2):
+                first_edge(buffer, edge_recv, m, c).start()
+
+            @pl.when(jnp.logical_not(moved))
+            def _():
+                buffer[m, :, pl.ds(1, rows)] = first[m]
 
     w_copy = pltpu.make_async_copy(weights, w, w_sem)
     w_copy.start()
@@ -238,13 +254,13 @@
     def _():
         for m in range(micros):
             for q in range(quarters):
-                local_in(images, xin, m, q).start()
+                local_in(images, m, q).start()
 
     @pl.when(stage == last)
     def _():
         for m in range(micros):
             for q in range(quarters):
-                local_in(cotangent, gin, m, q).start()
+                local_in(cotangent, m, q).start()
 
     barrier = pltpu.get_barrier_semaphore()
 
@@ -257,14 +273,14 @@
     @pl.when(stage > 0)
     def _():
         greet(stage - 1, sp, dp)
-        greet(stage - 1, osp, dp)
+        greet(stage - 1, sp, odp)
 
     @pl.when(stage < last)
     def _():
         greet(stage + 1, sp, dp)
-        greet(stage + 1, osp, dp)
-
-    zero_row = (rows + 1) * sp
+        greet(stage + 1, sp, odp)
+
+    zero_row = (rows + 1) * dp
     blank = jnp.zeros((micros, quarters, 1, cols, LANES), jnp.float32)
     xin[:, :, pl.ds(zero_row, 1)] = blank.astype(xin.dtype)
     gin[:, :, pl.ds(zero_row, 1)] = blank.astype(gin.dtype)
@@ -276,19 +292,11 @@
 
     @pl.when(stage == 0)
     def _():
-        for m in range(micros):
-            for q in range(quarters):
-                local_in(images, xin, m, q).wait()
-            for c in range(2):
-                x_first(m, c).start()
+        hand_out(images, xin, x_recv, xh_recv)
 
     @pl.when(stage == last)
     def _():
-        for m in range(micros):
-            for q in range(quarters):
-                local_in(cotangent, gin, m, q).wait()
-            for c in range(2):
-                g_first(m, c).start()
+        hand_out(cotangent, gin, g_recv, gh_recv)
 
     w_copy.wait()
 
@@ -327,7 +335,7 @@
 
     def forward(m):
         for c in range(2):
-            @pl.when(stage > 0)
+            @pl.when(jnp.logical_or(stage > 0, moved))
             def _():
                 x_main(m, c).wait_recv()
 
@@ -355,7 +363,7 @@
     def backward(m):
         slope_edge(m).wait_recv()
         for c in range(2):
-            @pl.when(stage < last)
+            @pl.when(jnp.logical_or(stage < last, moved))
             def _():
                 g_main(m, c).wait_recv()
 
@@ -383,11 +391,15 @@
                 g_main(m, n).start()
                 g_edge(m, n).start()
 
+        @pl.when(m > 0)
+        def _():
+            pass_on(m - 1)
+
     def prepare(m):
         for j in range(3):
             x_slice(m, j).wait_recv()
         for image in range(2):
-            tall = jnp.concatenate([xs[m, image], xs[m, 2 + image]], axis=0).astype(jnp.float32)
+            tall = jnp.concatenate([xs[m, 2 * image], xs[m, 2 * image + 1]], axis=0).astype(jnp.float32)
             blank_row = jnp.zeros((1, cols, LANES), jnp.float32)
             shifted = column_shifts(tall.reshape(2 * pixels, LANES))
             for b in range(3):
@@ -397,27 +409,33 @@
                     for a in range(3):
                         lo = part * rows + a
                         block = field[lo:lo + rows].reshape(pixels, LANES)
-                        xt[m, part, 3 * a + b, :, pl.ds(image * LANES, LANES)] = block.T.astype(
+                        xt[m, image, 3 * a + b, :, pl.ds(part * LANES, LANES)] = block.T.astype(
                             xt.dtype)
 
-    def add_grad(m, part):
+    def add_grad(m, image):
         blocks = []
-        for image in range(2):
+        for part in range(2):
             blocks.append(jnp.concatenate(
-                [dall[m, part * 2 + image, q] for q in range(quarters)], axis=-1))
+                [dall[m, image * 2 + part, q] for q in range(quarters)], axis=-1))
         rhs = jnp.concatenate(blocks, axis=0)
         for a in range(3):
-            lhs = xt[m, part, pl.ds(3 * a, 3)].reshape(3 * LANES, 2 * pixels)
+            lhs = xt[m, image, pl.ds(3 * a, 3)].reshape(3 * LANES, 2 * pixels)
             total = jnp.dot(lhs, rhs, preferred_element_type=jnp.float32)
             grad[pl.ds(3 * a, 3)] += total.reshape(3, LANES, chans)
 
+    def pass_on(m):
+        for c in range(2):
+            d_block(m, c, 1).wait_recv()
+            d_block(m, c, 2).start()
+
     def accumulate(m):
+        @pl.when(m == micros - 1)
+        def _():
+            pass_on(m)
+
         for c in range(2):
             d_block(m, c, 0).wait_recv()
         add_grad(m, sp)
-        for c in range(2):
-            d_block(m, c, 1).wait_recv()
-            d_block(m, c, 2).start()
         for c in range(2):
             d_block(m, c, 2).wait_recv()
         add_grad(m, osp)
@@ -473,18 +491,18 @@
                 x_main(m, c).wait_send()
                 x_edge(m, c).wait_send()
 
-            @pl.when(stage == 0)
-            def _():
-                x_first(m, c).wait_send()
-
             @pl.when(stage > 0)
             def _():
                 g_main(m, c).wait_send()
                 g_edge(m, c).wait_send()
 
-            @pl.when(stage == last)
-            def _():
-                g_first(m, c).wait_send()
+            @pl.when(jnp.logical_or(stage == 0, stage == last))
+            def _():
+                first_edge(xin, xh_recv, m, c).wait_send()
+
+                @pl.when(moved)
+                def _():
+                    first_main(xin, x_recv, m, c).wait_send()
 
     result.wait()
 
@@ -501,11 +519,12 @@
     grads = pl.pallas_call(
         pipeline_kernel,
         out_shape=jax.ShapeDtypeStruct((9, LANES, chans), f32),
-        in_specs=[pl.BlockSpec(memory_space=pl.ANY)] * 3,
+        in_specs=[pl.BlockSpec(memory_space=pltpu.HBM)] * 3,
         out_specs=pl.BlockSpec(memory_space=pl.ANY),
         scratch_shapes=[
             pltpu.VMEM((9, chans, chans), bf16),
             pltpu.VMEM((9, chans, chans), bf16),
+            pltpu.VMEM(plain, bf16),
             pltpu.VMEM(padded, bf16),
             pltpu.VMEM(plain, bf16),
             pltpu.VMEM(padded, bf16),
@@ -518,7 +537,7 @@
             pltpu.VMEM((2, rows + 2, cols, 3 * chans // 2), bf16),
             pltpu.VMEM((9, LANES, chans), f32),
             dma, dma((micros, quarters)), dma,
-            dma((micros, 2)),
+            dma((micros, 2)), dma((micros, 2)),
             dma((micros, 2)), dma((micros, 2)), dma((micros, 2)), dma((micros, 2)),
             dma((micros, 2)), dma((micros, 2)), dma((micros, 2)), dma((micros, 2)),
             dma((micros,)), dma((micros,)), dma((micros, 3)), dma((micros, 3)),

time: 118 us -> 115 us (0.975)
  Pallas kernels: 114 us -> 111 us
    pallas_call x1, Pallas kernels: 114 us -> 111 us  [kernel_shards(): pl.pallas_call(pipeline_kernel, out_shape=jax.ShapeDtypeStruct((9, LANES,...]
where the time goes in v2:
time: 115 us; the launch traced here: 114 us
  Pallas kernels  111 us (97%)
  local copies, waits for them, and re-layouts  3.49 us (3%)
    pallas_call x1, Pallas kernels, kernel_shards(): pl.pallas_call(pipeline_kernel, out_shape=jax.ShapeDtypeStruct((9, LANES,...  111 us
    unnamed x5, local copies, waits for them, and re-layouts  3.49 us

profile of v2, /device:TPU:1, one launch (start us, length us, event | category | flops | bytes accessed | tf_op | source)
XLA Modules:
  0.0 114.3 jit_solution(2856836032554905968)
XLA Ops:
  0.0 0.0 copy-start
  0.0 1.0 copy-done
  1.0 0.0 copy-start.1
  1.0 1.0 copy-done.1
  2.1 110.8 %shard_map.37 = f32[9,128,512]{2,1,0:T(8,128)S(1)} custom-call(bf16[4,8,16,512]{3,2,1,0:T(8,128)(2,1)S(1)} %bitcast.5, bf16[4,8,16,512]{3,2,1,0:T(8,128)(2,1)S(1)} %bitcast.6, bf16[9,512,512]{2,1,0:T(8,128)(2,1)} %bitcast.7), custom_call_target="tpu_custom_call" | custom-call | flops 7247757312 | bytes 9437184 | tf_op jit(solution)/shard_map/pallas_call | solution.py:519
  112.9 1.4 %copy.5 = f32[1,9,128,512]{3,2,1,0:T(8,128)} copy(f32[1,9,128,512]{3,2,1,0:T(8,128)S(1)} %bitcast.4) | data formatting | bytes 4718592
Async XLA Ops:
  0.0 1.0 copy-start
  1.0 1.0 copy-start.1

commit v3 on v1

--- a/solution.py
+++ b/solution.py
@@ -343,8 +343,8 @@
 
             @pl.when(stage < last)
             def _():
+                x_edge(m, n).start()
                 x_main(m, n).start()
-                x_edge(m, n).start()
 
             store_half(slope, m, n, 1, sig * (1.0 + z * (1.0 - sig)))
         slope_edge(m).start()
@@ -371,8 +371,10 @@
                 if c == 0:
                     acc[...] = product(wt, 0, 0, chans)
 
-            d_block(m, c, 1).start()
-            d_block(m, c, 0).start()
+            @pl.when(stage == 0)
+            def _():
+                d_block(m, c, 1).start()
+                d_block(m, c, 0).start()
 
         @pl.when(stage > 0)
         def _():
@@ -380,8 +382,15 @@
                 own = load_half(gin, m, n)[1:rows + 1].reshape(pixels, half)
                 flow = acc[:, pl.ds(n * half, half)] + product(wt, 1, n * half, half)
                 store_half(gout, m, n, 0, own + flow)
+                g_edge(m, n).start()
                 g_main(m, n).start()
-                g_edge(m, n).start()
+            for c in range(2):
+                d_block(m, c, 1).start()
+                d_block(m, c, 0).start()
+
+        @pl.when(m > 0)
+        def _():
+            pass_on(m - 1)
 
     def prepare(m):
         for j in range(3):
@@ -411,13 +420,19 @@
             total = jnp.dot(lhs, rhs, preferred_element_type=jnp.float32)
             grad[pl.ds(3 * a, 3)] += total.reshape(3, LANES, chans)
 
+    def pass_on(m):
+        for c in range(2):
+            d_block(m, c, 1).wait_recv()
+            d_block(m, c, 2).start()
+
     def accumulate(m):
+        @pl.when(m == micros - 1)
+        def _():
+            pass_on(m)
+
         for c in range(2):
             d_block(m, c, 0).wait_recv()
         add_grad(m, sp)
-        for c in range(2):
-            d_block(m, c, 1).wait_recv()
-            d_block(m, c, 2).start()
         for c in range(2):
             d_block(m, c, 2).wait_recv()
         add_grad(m, osp)
@@ -428,7 +443,7 @@
         early += [B[i], W[i - 1]]
     early += [W[-1]]
     late = F + B + Q + W
-    final = [v for pair in zip(F, B) for v in pair] + Q + W
+    final = [F[0]] + [v for pair in zip(F[1:], B) for v in pair] + [B[-1]] + Q + W
 
     @pl.loop(0, 4 * micros)
     def _(step):
@@ -501,7 +516,7 @@
     grads = pl.pallas_call(
         pipeline_kernel,
         out_shape=jax.ShapeDtypeStruct((9, LANES, chans), f32),
-        in_specs=[pl.BlockSpec(memory_space=pl.ANY)] * 3,
+        in_specs=[pl.BlockSpec(memory_space=pltpu.HBM)] * 3,
         out_specs=pl.BlockSpec(memory_space=pl.ANY),
         scratch_shapes=[
             pltpu.VMEM((9, chans, chans), bf16),

time: 118 us -> 115 us (0.975)
  Pallas kernels: 114 us -> 112 us
    pallas_call x1, Pallas kernels: 114 us -> 112 us  [kernel_shards(): pl.pallas_call(pipeline_kernel, out_shape=jax.ShapeDtypeStruct((9, LANES,...]
where the time goes in v3:
time: 115 us
  Pallas kernels  112 us (97%)
  local copies, waits for them, and re-layouts  3.49 us (3%)
    pallas_call x1, Pallas kernels, kernel_shards(): pl.pallas_call(pipeline_kernel, out_shape=jax.ShapeDtypeStruct((9, LANES,...  112 us
    unnamed x5, local copies, waits for them, and re-layouts  3.49 us

profile of v3, /device:TPU:1, one launch (start us, length us, event | category | flops | bytes accessed | tf_op | source)
XLA Modules:
  0.0 115.2 jit_solution(4064627276559486054)
XLA Ops:
  0.0 0.0 copy-start
  0.0 1.0 copy-done
  1.0 0.0 copy-start.1
  1.0 1.0 copy-done.1
  2.1 111.7 %shard_map.37 = f32[9,128,512]{2,1,0:T(8,128)S(1)} custom-call(bf16[4,8,16,512]{3,2,1,0:T(8,128)(2,1)S(1)} %bitcast.5, bf16[4,8,16,512]{3,2,1,0:T(8,128)(2,1)S(1)} %bitcast.6, bf16[9,512,512]{2,1,0:T(8,128)(2,1)} %bitcast.7), custom_call_target="tpu_custom_call" | custom-call | flops 7247757312 | bytes 9437184 | tf_op jit(solution)/shard_map/pallas_call | solution.py:516
  113.8 1.4 %copy.5 = f32[1,9,128,512]{3,2,1,0:T(8,128)} copy(f32[1,9,128,512]{3,2,1,0:T(8,128)S(1)} %bitcast.4) | data formatting | bytes 4718592
Async XLA Ops:
  0.0 1.0 copy-start
  1.0 1.0 copy-start.1

commit v4 on v2

--- a/solution.py
+++ b/solution.py
@@ -351,8 +351,8 @@
 
             @pl.when(stage < last)
             def _():
+                x_edge(m, n).start()
                 x_main(m, n).start()
-                x_edge(m, n).start()
 
             store_half(slope, m, n, 1, sig * (1.0 + z * (1.0 - sig)))
         slope_edge(m).start()
@@ -388,8 +388,8 @@
                 own = load_half(gin, m, n)[1:rows + 1].reshape(pixels, half)
                 flow = acc[:, pl.ds(n * half, half)] + product(wt, 1, n * half, half)
                 store_half(gout, m, n, 0, own + flow)
+                g_edge(m, n).start()
                 g_main(m, n).start()
-                g_edge(m, n).start()
 
         @pl.when(m > 0)
         def _():

time: 115 us -> 109 us (0.948)
  Pallas kernels: 111 us -> 105 us
    pallas_call x1, Pallas kernels: 111 us -> 105 us  [kernel_shards(): pl.pallas_call(pipeline_kernel, out_shape=jax.ShapeDtypeStruct((9, LANES,...]
where the time goes in v4:
time: 109 us
  Pallas kernels  105 us (96%)
  local copies, waits for them, and re-layouts  3.49 us (3%)
    pallas_call x1, Pallas kernels, kernel_shards(): pl.pallas_call(pipeline_kernel, out_shape=jax.ShapeDtypeStruct((9, LANES,...  105 us
    unnamed x5, local copies, waits for them, and re-layouts  3.49 us

profile of v4, /device:TPU:1, one launch (start us, length us, event | category | flops | bytes accessed | tf_op | source)
XLA Modules:
  0.0 108.6 jit_solution(10470415664642027194)
XLA Ops:
  0.0 0.0 copy-start
  0.0 1.0 copy-done
  1.0 0.0 copy-start.1
  1.0 1.0 copy-done.1
  2.1 105.1 %shard_map.37 = f32[9,128,512]{2,1,0:T(8,128)S(1)} custom-call(bf16[4,8,16,512]{3,2,1,0:T(8,128)(2,1)S(1)} %bitcast.5, bf16[4,8,16,512]{3,2,1,0:T(8,128)(2,1)S(1)} %bitcast.6, bf16[9,512,512]{2,1,0:T(8,128)(2,1)} %bitcast.7), custom_call_target="tpu_custom_call" | custom-call | flops 7247757312 | bytes 9437184 | tf_op jit(solution)/shard_map/pallas_call | solution.py:519
  107.2 1.4 %copy.5 = f32[1,9,128,512]{3,2,1,0:T(8,128)} copy(f32[1,9,128,512]{3,2,1,0:T(8,128)S(1)} %bitcast.4) | data formatting | bytes 4718592
Async XLA Ops:
  0.0 1.0 copy-start
  1.0 1.0 copy-start.1
